TPU v7x, 128 devices: a whole 4x4x4 slice. The times are simulated.
128 devices in a mesh: dom: 16 (over z, y_lo, core), band: 8 (over x, y_hi).
Axes of the slice: x: 4, y: 4 (y_hi: 2, y_lo: 2; y = y_hi * 2 + y_lo), z: 4, core: 2. Of those that a mesh axis runs over, the one named last changes fastest.
Arguments:
- wavefunctions: bfloat16 [39168, 1024], P('dom', 'band')
- cell_hamiltonian: bfloat16 [512, 125, 125], P('dom')
- cell_nodes: int32 [512, 125], P('dom'), may hold values from 0 to 2600, as said below
- face_nodes: int32 [2448], P('dom'), may hold values from 0 to 2447, as said below
Outputs:
- filtered: bfloat16 [39168, 1024], P('dom', 'band')
- correlation: float32 [1024, 1024], P('dom', 'band')
- projected: float32 [1024, 1024], P('dom', 'band')
Inputs may be any that keep to these rules, and one draw needn't show every extreme that they name: `cell_nodes`: cells come in 16 runs of 32, one run a domain. Cell r of a run sits at x = r mod 2, y = (r div 2) mod 4, z = r div (8) of the domain's grid of cells, and its slot a = i + 5 j + 25 k names grid node (4 x + i, 4 y + j, 4 z + k) of the domain's grid of nodes. Grid nodes whose third coordinate is below 16 are the domain's own nodes, one local number each, all distinct. Node (p, q, 16) is named 2448 + q * 9 + p. `face_nodes`: entry f of a domain's 153 entries is the local number of its grid node (f mod (9), f div (9), 0) in the grid of cell_nodes.
All inputs are finite; a program needn't handle non-finite values.
Results may differ from a plain program's by a relative error of at most 0.013.
Values may be sent and summed in bfloat16 or wider, within the bound.
A program may use at most 64 MiB of HBM per device.

v0:
```python
import jax
import jax.numpy as jnp
import numpy as np
from jax import lax
from jax.experimental import pallas as pl
from jax.experimental.pallas import tpu as pltpu
from jax.sharding import PartitionSpec as P

CX, CY, CZ = 2, 4, 4
LINE = 4 * CX + 1
COL = 4 * CY + 1
PLANE = LINE * COL
OWN = 4 * CZ * PLANE
FACE_PAD = 160
GRID = OWN + FACE_PAD
RUN = 5 * LINE
RUN_PAD = 48
PAIR = 5 * RUN_PAD
PAIRS = CY * CZ
LAYER = 4 * PLANE
SLAB = 768
NX = 4
WAVE = 128
SORTED = 2560

filter_center = 1.0
filter_half = 1.5

f32 = jnp.float32
bf16 = jnp.bfloat16
MESH = pl.DeviceIdType.MESH


def expansion():
    e = np.zeros((PAIR, 2 * 128), np.float32)
    for k in range(5):
        for j in range(5):
            for x in range(LINE):
                for cell in range(CX):
                    i = x - 4 * cell
                    if 0 <= i < 5:
                        e[RUN_PAD * k + LINE * j + x, 128 * cell + i + 5 * j + 25 * k] = 1
    return e


def kernel(
    w_ref,
    h_ref,
    nodes_ref,
    e_ref,
    et_ref,
    filtered_ref,
    corr_ref,
    proj_ref,
    w32,
    ident,
    order,
    start,
    section,
    total,
    pairs,
    face_out,
    face_in,
    back_out,
    back_in,
    slabs,
    waves,
    compact,
    restored,
    piece,
    image,
    right,
    gram,
    from_core,
    half,
    from_x,
    quarter,
    final,
    face_s,
    face_r,
    back_s,
    back_r,
    x_s,
    x_r,
    y_s,
    y_r,
    core_s,
    core_r,
    red_s,
    red_r,
    fin_s,
    fin_r,
    out_s,
):
    d = lax.axis_index("dom")
    b = lax.axis_index("band")
    n_dom = lax.axis_size("dom")
    chip = lax.div(d, 2)
    core = lax.rem(d, 2)
    x = lax.div(b, 2)
    yh = lax.rem(b, 2)
    yl = lax.rem(chip, 2)
    prev = lax.rem(d + n_dom - 1, n_dom)
    succ = lax.rem(d + 1, n_dom)
    mate = (2 * chip + 1 - core, b)
    across = (d, 2 * x + 1 - yh)

    def along_x(xx):
        return (d, 2 * xx + yh)

    def other_chip(cc):
        return (2 * cc + core, b)

    barrier = pltpu.get_barrier_semaphore()
    greeted = [(prev, b), (succ, b), mate, across]
    greeted += [along_x(lax.rem(x + off, NX)) for off in range(1, NX)]
    greeted += [other_chip(lax.rem(chip + off, 8)) for off in range(1, 8)]
    for device in greeted:
        pl.semaphore_signal(barrier, inc=1, device_id=device, device_id_type=MESH)

    w32[...] = w_ref[...].astype(f32)

    def gather_plane(zz, carry):
        cz = lax.div(zz, 4)
        k = zz - 4 * cz
        for q in range(COL):
            cy = min(q // 4, CY - 1)
            for p in range(LINE):
                cx = min(p // 4, CX - 1)
                slot = (p - 4 * cx) + 5 * (q - 4 * cy)
                node = nodes_ref[cz * (CX * CY) + cy * CX + cx, slot + 25 * k]
                row = zz * PLANE + q * LINE + p
                start[pl.ds(row, 1), :] = w32[pl.ds(node, 1), :]
                ident[pl.ds(row, 1), :] = jnp.full((1, WAVE), node, jnp.int32)
        return carry

    lax.fori_loop(0, 4 * CZ, gather_plane, 0)
    pl.semaphore_wait(barrier, len(greeted))

    def face_copy(n):
        return pltpu.make_async_remote_copy(
            src_ref=face_out.at[n],
            dst_ref=face_in.at[n],
            send_sem=face_s.at[n],
            recv_sem=face_r.at[n],
            device_id=(prev, b),
            device_id_type=MESH,
        )

    def back_copy(n):
        return pltpu.make_async_remote_copy(
            src_ref=back_out.at[n],
            dst_ref=back_in.at[n],
            send_sem=back_s.at[n],
            recv_sem=back_r.at[n],
            device_id=(succ, b),
            device_id_type=MESH,
        )

    def send_face(n, field):
        face_out[n] = field[0:FACE_PAD, :].astype(bf16)
        face_copy(n).start()

    def take_face(n, field):
        face_copy(n).wait_recv()
        field[OWN:GRID, :] = face_in[n].astype(f32)

    def add_pair(block, base, source, target):
        rows = [source[base + PLANE * k : base + PLANE * k + RUN_PAD, :] for k in range(5)]
        rows = [r.astype(bf16) for r in rows] + [jnp.zeros((16, WAVE), bf16)]
        result = jnp.dot(block, jnp.concatenate(rows, axis=0), preferred_element_type=f32)
        for k in range(5):
            at = base + PLANE * k
            target[at : at + RUN_PAD, :] += result[RUN_PAD * k : RUN_PAD * (k + 1)]

    def clear(ref):
        def tile(i, carry):
            ref[pl.ds(pl.multiple_of(16 * i, 16), 16), :] = jnp.zeros((16, WAVE), f32)
            return carry

        lax.fori_loop(0, ref.shape[0] // 16, tile, 0)

    def add_layer(cz, source):
        for cy in range(CY):
            add_pair(pairs[CY * cz + cy], LAYER * cz + 4 * LINE * cy, source, total)

    send_face(0, start)

    for p in range(PAIRS):
        block = None
        for cell in range(CX):
            at = 128 * cell
            rows = jnp.dot(
                e_ref[:, at : at + 125], h_ref[CX * p + cell], preferred_element_type=f32
            ).astype(bf16)
            part = jnp.dot(rows, et_ref[at : at + 125, :], preferred_element_type=f32)
            block = part if block is None else block + part
        pairs[p] = block.astype(bf16)

    def first_half(n, source):
        clear(total)
        add_layer(0, source)
        add_layer(1, source)
        take_face(n, source)
        add_layer(3, source)
        back_out[n] = total[OWN:GRID, :]
        back_copy(n).start()
        add_layer(2, source)

    def take_back(n):
        back_copy(n).wait_recv()
        total[0:FACE_PAD, :] += back_in[n]

    def to_section(lo, hi):
        value = (total[lo:hi, :] - filter_center * start[lo:hi, :]) * (1.0 / filter_half)
        section[lo:hi, :] = value.astype(bf16).astype(f32)

    def to_filtered(lo, hi):
        value = (total[lo:hi, :] - filter_center * section[lo:hi, :]) * (2.0 / filter_half)
        value = (value - start[lo:hi, :]).astype(bf16)
        compact[lo:hi, :] = value
        start[lo:hi, :] = value.astype(f32)

    first_half(0, start)
    to_section(FACE_PAD, OWN)
    take_back(0)
    to_section(0, FACE_PAD)
    send_face(1, section)
    first_half(1, section)
    to_filtered(FACE_PAD, OWN)

    def x_copy(j):
        return pltpu.make_async_remote_copy(
            src_ref=slabs.at[j],
            dst_ref=waves.at[x],
            send_sem=x_s.at[j],
            recv_sem=x_r.at[x],
            device_id=along_x(j),
            device_id_type=MESH,
        )

    def x_arrival(xx):
        return pltpu.make_async_remote_copy(
            src_ref=slabs.at[0],
            dst_ref=waves.at[xx],
            send_sem=x_s.at[0],
            recv_sem=x_r.at[xx],
            device_id=along_x(xx),
            device_id_type=MESH,
        )

    def y_copy(xx):
        return pltpu.make_async_remote_copy(
            src_ref=waves.at[xx],
            dst_ref=waves.at[NX + xx],
            send_sem=y_s.at[xx],
            recv_sem=y_r.at[xx],
            device_id=across,
            device_id_type=MESH,
        )

    def send_slab(j):
        slabs[j] = start[LAYER * j : LAYER * j + SLAB, :].astype(bf16)

        @pl.when(x != j)
        def _():
            x_copy(j).start()

        @pl.when(x == j)
        def _():
            waves[j] = slabs[j]
            y_copy(j).start()

    send_slab(1)
    send_slab(2)
    take_back(1)
    to_filtered(0, FACE_PAD)
    send_face(2, start)
    send_slab(0)
    take_face(2, start)
    send_slab(3)

    compact[OWN:SORTED, :] = jnp.zeros((SORTED - OWN, WAVE), bf16)
    ident[OWN:SORTED, :] = jnp.full((SORTED - OWN, WAVE), -1, jnp.int32)
    for t in range(SORTED // WAVE):
        order[:, WAVE * t : WAVE * (t + 1)] = ident[WAVE * t : WAVE * (t + 1), :].T[:8]

    def restore(lo, hi):
        rows = lax.broadcasted_iota(jnp.int32, (hi - lo, 256), 0) + lo
        value = jnp.zeros((hi - lo, WAVE), f32)
        for t in range(SORTED // 256):
            here = jnp.broadcast_to(order[0:1, 256 * t : 256 * (t + 1)], (hi - lo, 256))
            hit = jnp.where(rows == here, 1.0, 0.0).astype(bf16)
            value += jnp.dot(hit, compact[256 * t : 256 * (t + 1), :], preferred_element_type=f32)
        restored[lo:hi, :] = value.astype(bf16)

    def out_copy():
        return pltpu.make_async_copy(restored, filtered_ref, out_s)

    own_rows = lax.broadcasted_iota(jnp.int32, (SLAB, WAVE), 0) < LAYER

    def take_piece(xx):
        piece[...] = waves[xx].astype(f32)
        clear(image)
        for cy in range(CY):
            add_pair(pairs[CY * x + cy], 4 * LINE * cy, piece, image)
        at = pl.multiple_of(2 * WAVE * xx, 2 * WAVE)
        right[:, pl.ds(at, WAVE)] = jnp.where(own_rows, piece[...], 0.0).astype(bf16)
        right[:, pl.ds(at + WAVE, WAVE)] = image[...].astype(bf16)

    take_piece(x)
    restore(0, 640)
    for off, lo, hi in ((1, 640, 1280), (3, 1280, 1920), (2, 1920, OWN)):
        xx = lax.rem(x + off, NX)
        x_arrival(xx).wait_recv()
        y_copy(xx).start()
        take_piece(xx)
        restore(lo, hi)
    out_copy().start()

    keep = pl.multiple_of(64 * core, 64)
    give = pl.multiple_of(64 * (1 - core), 64)

    def core_copy(t):
        return pltpu.make_async_remote_copy(
            src_ref=gram.at[t, pl.ds(give, 64)],
            dst_ref=from_core.at[t],
            send_sem=core_s.at[t],
            recv_sem=core_r.at[t],
            device_id=mate,
            device_id_type=MESH,
        )

    def block_of(xx):
        return pl.ds(pl.multiple_of(2 * WAVE * xx, 2 * WAVE), 2 * WAVE)

    def red_copy(t, xx):
        return pltpu.make_async_remote_copy(
            src_ref=half.at[t, :, block_of(xx)],
            dst_ref=from_x.at[t, x],
            send_sem=red_s.at[t, xx],
            recv_sem=red_r.at[t, x],
            device_id=along_x(xx),
            device_id_type=MESH,
        )

    def red_arrival(t, xx):
        return pltpu.make_async_remote_copy(
            src_ref=half.at[t, :, block_of(xx)],
            dst_ref=from_x.at[t, xx],
            send_sem=red_s.at[t, xx],
            recv_sem=red_r.at[t, xx],
            device_id=along_x(xx),
            device_id_type=MESH,
        )

    def target_chip(t):
        band_side = jnp.where(t < NX, yh, 1 - yh)
        return 2 * lax.rem(t, NX) + band_side

    def fin_copy(t):
        return pltpu.make_async_remote_copy(
            src_ref=quarter.at[t],
            dst_ref=final.at[chip],
            send_sem=fin_s.at[t],
            recv_sem=fin_r.at[chip],
            device_id=other_chip(target_chip(t)),
            device_id_type=MESH,
        )

    def fin_arrival(cc):
        return pltpu.make_async_remote_copy(
            src_ref=quarter.at[0],
            dst_ref=final.at[cc],
            send_sem=fin_s.at[0],
            recv_sem=fin_r.at[cc],
            device_id=other_chip(cc),
            device_id_type=MESH,
        )

    def multiply(t):
        gram[t] = lax.dot_general(
            waves[t], right[...], (((0,), (0,)), ((), ())), preferred_element_type=f32
        ).astype(bf16)
        core_copy(t).start()

    def sum_core(t):
        core_copy(t).wait_recv()
        value = gram[t, pl.ds(keep, 64), :].astype(f32) + from_core[t].astype(f32)
        half[t] = value.astype(bf16)
        for off in range(1, NX):
            red_copy(t, lax.rem(x + off, NX)).start()

    def sum_x(t):
        value = half[t, :, block_of(x)].astype(f32)
        for off in range(1, NX):
            xx = lax.rem(x + off, NX)
            red_arrival(t, xx).wait_recv()
            value += from_x[t, xx].astype(f32)
        quarter[t] = value.astype(bf16)
        away = target_chip(t) != chip

        @pl.when(away)
        def _():
            fin_copy(t).start()

        @pl.when(jnp.logical_not(away))
        def _():
            final[chip] = quarter[t]

    def band_round(t, carry):
        @pl.when(jnp.logical_and(t >= NX, t < 2 * NX))
        def _():
            y_copy(t - NX).wait_recv()

        @pl.when(t < 2 * NX)
        def _():
            multiply(t)

        @pl.when(jnp.logical_and(t >= 1, t < 2 * NX + 1))
        def _():
            sum_core(t - 1)

        @pl.when(t >= 2)
        def _():
            sum_x(t - 2)

        return carry

    lax.fori_loop(0, 2 * NX + 2, band_round, 0)

    for cc in range(8):

        @pl.when(chip != cc)
        def _():
            fin_arrival(cc).wait_recv()

    result = final[0].astype(f32)
    for cc in range(1, 8):
        result += final[cc].astype(f32)
    result = result * (1.0 / (n_dom * OWN))
    corr_ref[...] = result[:, :WAVE]
    proj_ref[...] = result[:, WAVE:]

    for n in range(3):
        face_copy(n).wait_send()
    for n in range(2):
        back_copy(n).wait_send()
    for j in range(NX):

        @pl.when(x != j)
        def _():
            x_copy(j).wait_send()

        y_copy(j).wait_send()

    def drain(t, carry):
        core_copy(t).wait_send()
        for off in range(1, NX):
            red_copy(t, lax.rem(x + off, NX)).wait_send()

        @pl.when(target_chip(t) != chip)
        def _():
            fin_copy(t).wait_send()

        return carry

    lax.fori_loop(0, 2 * NX, drain, 0)
    out_copy().wait()


def shards(wavefunctions, cell_hamiltonian, cell_nodes, face_nodes):
    e = expansion()
    expand = jnp.asarray(e, bf16)
    expand_t = jnp.asarray(np.pad(e.T, ((0, 0), (0, 256 - PAIR))), bf16)
    vmem = pl.BlockSpec(memory_space=pltpu.VMEM)
    dma = pltpu.SemaphoreType.DMA
    return pl.pallas_call(
        kernel,
        out_shape=(
            jax.ShapeDtypeStruct((OWN, WAVE), bf16),
            jax.ShapeDtypeStruct((64, WAVE), f32),
            jax.ShapeDtypeStruct((64, WAVE), f32),
        ),
        in_specs=[vmem, vmem, pl.BlockSpec(memory_space=pltpu.SMEM), vmem, vmem],
        out_specs=(pl.BlockSpec(memory_space=pl.ANY), vmem, vmem),
        scratch_shapes=[
            pltpu.VMEM((OWN, WAVE), f32),
            pltpu.VMEM((SORTED, WAVE), jnp.int32),
            pltpu.VMEM((8, SORTED), jnp.int32),
            pltpu.VMEM((GRID, WAVE), f32),
            pltpu.VMEM((GRID, WAVE), f32),
            pltpu.VMEM((GRID, WAVE), f32),
            pltpu.VMEM((PAIRS, PAIR, 256), bf16),
            pltpu.VMEM((3, FACE_PAD, WAVE), bf16),
            pltpu.VMEM((3, FACE_PAD, WAVE), bf16),
            pltpu.VMEM((2, FACE_PAD, WAVE), f32),
            pltpu.VMEM((2, FACE_PAD, WAVE), f32),
            pltpu.VMEM((NX, SLAB, WAVE), bf16),
            pltpu.VMEM((2 * NX, SLAB, WAVE), bf16),
            pltpu.VMEM((SORTED, WAVE), bf16),
            pltpu.VMEM((OWN, WAVE), bf16),
            pltpu.VMEM((SLAB, WAVE), f32),
            pltpu.VMEM((SLAB, WAVE), f32),
            pltpu.VMEM((SLAB, 2 * NX * WAVE), bf16),
            pltpu.VMEM((2 * NX, WAVE, 2 * NX * WAVE), bf16),
            pltpu.VMEM((2 * NX, 64, 2 * NX * WAVE), bf16),
            pltpu.VMEM((2 * NX, 64, 2 * NX * WAVE), bf16),
            pltpu.VMEM((2 * NX, NX, 64, 2 * WAVE), bf16),
            pltpu.VMEM((2 * NX, 64, 2 * WAVE), bf16),
            pltpu.VMEM((8, 64, 2 * WAVE), bf16),
            dma((3,)),
            dma((3,)),
            dma((2,)),
            dma((2,)),
            dma((NX,)),
            dma((NX,)),
            dma((NX,)),
            dma((NX,)),
            dma((2 * NX,)),
            dma((2 * NX,)),
            dma((2 * NX, NX)),
            dma((2 * NX, NX)),
            dma((2 * NX,)),
            dma((8,)),
            dma,
        ],
        compiler_params=pltpu.CompilerParams(
            collective_id=0, has_side_effects=True, vmem_limit_bytes=48 << 20
        ),
        name="chebyshev_filter",
    )(wavefunctions, cell_hamiltonian, cell_nodes, expand, expand_t)


def solution(mesh):
    placed = (P("dom", "band"), P("dom", None, None), P("dom", None), P("dom"))
    return jax.shard_map(
        shards,
        mesh=mesh,
        in_specs=placed,
        out_specs=(P("dom", "band"), P("dom", "band"), P("dom", "band")),
        check_vma=False,
    )
```

profile of v0, /device:TPU:112, one launch (start us, length us, event | category | flops | bytes accessed | tf_op | source)
XLA Modules:
  0.0 69.6 jit_solution(17096872990302483050)
XLA Ops:
  0.6 0.0 copy-start.1
  0.6 0.0 copy-start.2
  0.7 0.0 copy-start.3
  0.7 0.0 copy-start
  0.7 1.7 %copy.8.h_ref = bf16[32,125,125]{2,1,0:T(8,128)(2,1)S(1)} copy(bf16[32,125,125]{2,0,1:T(8,128)(2,1)} %param.7) | data formatting | bytes 2000000 | tf_op args[1]
  2.4 0.0 copy-done.1
  2.4 0.0 copy-done.2
  2.4 0.0 copy-done.3
  2.4 0.0 copy-done
  2.4 65.1 %chebyshev_filter.1 = (bf16[2448,128]{1,0:T(8,128)(2,1)S(1)}, f32[64,128]{1,0:T(8,128)S(1)}, f32[64,128]{1,0:T(8,128)S(1)}) custom-call(bf16[2448,128]{1,0:T(8,128)(2,1)S(1)} %copy-done, bf16[32,125,125]{2,1,0:T(8,128)(2,1)S(1)} %copy.8.h_ref, s32[32,125]{1,0:T(8,128)S(1)} %copy-done.3, bf16[240,256]{1,0:T(8,128)(2,1)S(1)} %copy-done.2, ...), custom_call_target="tpu_custom_call" | custom-call | tf_op jit(solution)/shard_map/chebyshev_filter/pallas_call | solution.py:478
  67.6 0.8 %copy.12 = bf16[2448,128]{1,0:T(8,128)(2,1)} copy(bf16[2448,128]{1,0:T(8,128)(2,1)S(1)} %get-tuple-element.6) | data formatting | bytes 1253376
  68.4 0.6 copy.13
  69.0 0.6 copy.14
Async XLA Ops:
  0.6 1.7 %copy-start.1 = (bf16[256,256]{1,0:T(8,128)(2,1)S(1)}, bf16[256,256]{1,0:T(8,128)(2,1)}, u32[]{:S(2)}) copy-start(bf16[256,256]{1,0:T(8,128)(2,1)} %constant.5.clone.et_ref) | copy-start | bytes 393220
  0.6 1.7 %copy-start.2 = (bf16[240,256]{1,0:T(8,128)(2,1)S(1)}, bf16[240,256]{1,0:T(8,128)(2,1)}, u32[]{:S(2)}) copy-start(bf16[240,256]{1,0:T(8,128)(2,1)} %constant.4.clone.e_ref) | copy-start | bytes 368644
  0.7 1.7 %copy-start.3 = (s32[32,125]{1,0:T(8,128)S(1)}, s32[32,125]{1,0:T(8,128)}, u32[]{:S(2)}) copy-start(s32[32,125]{1,0:T(8,128)} %nodes_ref.1) | copy-start | bytes 48004
  0.7 1.7 %copy-start = (bf16[2448,128]{1,0:T(8,128)(2,1)S(1)}, bf16[2448,128]{1,0:T(8,128)(2,1)}, u32[]{:S(2)}) copy-start(bf16[2448,128]{1,0:T(8,128)(2,1)} %w_ref.1) | copy-start | bytes 1880068
where the time goes:
time: 69.8 us; the launch traced here: 69.6 us
  Pallas kernels  65.1 us (93%)
  local copies, waits for them, and re-layouts  3.77 us (5%)
  between operations  0.7 us (1%)
    pallas_call x1, Pallas kernels, shards(): pl.pallas_call(kernel, out_shape=(jax.ShapeDtypeStruct((OWN, WAVE), bf16)...  65.1 us
    unnamed x12, local copies, waits for them, and re-layouts  3.77 us

commit v1 on v0

v1 whole, which is shorter than its diff:
```python
import jax
import jax.numpy as jnp
import numpy as np
from jax import lax
from jax.experimental import pallas as pl
from jax.experimental.pallas import tpu as pltpu
from jax.sharding import PartitionSpec as P

CX, CY, CZ = 2, 4, 4
LINE = 4 * CX + 1
COL = 4 * CY + 1
PLANE = LINE * COL
OWN = 4 * CZ * PLANE
FACE_PAD = 160
GRID = OWN + FACE_PAD
TOTAL = 2688
RUN = 5 * LINE
RUN_PAD = 48
PAIR = 5 * RUN_PAD
PAIRS = CY * CZ
LAYER = 4 * PLANE
SLAB = 768
EARLY = SLAB - FACE_PAD
ACROSS = EARLY + 16
NX = 4
WAVE = 128
SORTED = 2560

filter_center = 1.0
filter_half = 1.5

f32 = jnp.float32
bf16 = jnp.bfloat16
MESH = pl.DeviceIdType.MESH


def expansion():
    e = np.zeros((PAIR, 2 * 128), np.float32)
    for k in range(5):
        for j in range(5):
            for x in range(LINE):
                for cell in range(CX):
                    i = x - 4 * cell
                    if 0 <= i < 5:
                        e[RUN_PAD * k + LINE * j + x, 128 * cell + i + 5 * j + 25 * k] = 1
    return e


def kernel(
    w_ref,
    h_ref,
    nodes_ref,
    e_ref,
    et_ref,
    filtered_ref,
    sums_ref,
    w32,
    h32,
    ident,
    order,
    start,
    section,
    total,
    pairs,
    face_out,
    face_in,
    back_out,
    back_in,
    corner,
    edge_out,
    edge_in,
    slabs,
    waves,
    compact,
    restored,
    piece,
    image,
    right,
    gram,
    from_core,
    half,
    from_x,
    quarter,
    final,
    face_s,
    face_r,
    back_s,
    back_r,
    corner_s,
    corner_r,
    edge_s,
    edge_r,
    x_s,
    x_r,
    y_s,
    y_r,
    core_s,
    core_r,
    red_s,
    red_r,
    fin_s,
    fin_r,
    out_s,
):
    d = lax.axis_index("dom")
    b = lax.axis_index("band")
    n_dom = lax.axis_size("dom")
    chip = lax.div(d, 2)
    core = lax.rem(d, 2)
    x = lax.div(b, 2)
    yh = lax.rem(b, 2)
    yl = lax.rem(chip, 2)
    prev = lax.rem(d + n_dom - 1, n_dom)
    succ = lax.rem(d + 1, n_dom)
    mate = (2 * chip + 1 - core, b)
    across = (d, 2 * x + 1 - yh)

    next_layer = (jnp.where(x == NX - 1, succ, d), 2 * lax.rem(x + 1, NX) + yh)

    def along_x(xx):
        return (d, 2 * xx + yh)

    def other_chip(cc):
        return (2 * cc + core, b)

    barrier = pltpu.get_barrier_semaphore()
    greeted = [(prev, b), (succ, b), mate, across, next_layer]
    greeted += [along_x(lax.rem(x + off, NX)) for off in range(1, NX)]
    greeted += [other_chip(lax.rem(chip + off, 8)) for off in range(1, 8)]
    for device in greeted:
        pl.semaphore_signal(barrier, inc=1, device_id=device, device_id_type=MESH)

    def face_copy(n):
        return pltpu.make_async_remote_copy(
            src_ref=face_out.at[n],
            dst_ref=face_in.at[n],
            send_sem=face_s.at[n],
            recv_sem=face_r.at[n],
            device_id=(prev, b),
            device_id_type=MESH,
        )

    def back_copy(n):
        return pltpu.make_async_remote_copy(
            src_ref=back_out.at[n],
            dst_ref=back_in.at[n],
            send_sem=back_s.at[n],
            recv_sem=back_r.at[n],
            device_id=(succ, b),
            device_id_type=MESH,
        )

    once = 1 + lax.div(d, n_dom)

    def apart(body):
        def step(i, carry):
            body()
            return carry

        lax.fori_loop(0, once, step, 0)

    def send_face(n, field):
        face_out[n] = field[0:FACE_PAD, :].astype(bf16)
        face_copy(n).start()

    def take_face(n, field):
        face_copy(n).wait_recv()

        @apart
        def _():
            field[OWN:GRID, :] = face_in[n].astype(f32)

    corner_copy = pltpu.make_async_remote_copy(
        src_ref=pairs.at[pl.ds(PAIRS - CY, CY), pl.ds(4 * RUN_PAD, RUN_PAD)],
        dst_ref=corner,
        send_sem=corner_s,
        recv_sem=corner_r,
        device_id=(succ, b),
        device_id_type=MESH,
    )

    def add_pair(block, base, source, target, used=range(5), kept=range(5)):
        rows = []
        for k in range(5):
            if k in used:
                rows.append(source[base + PLANE * k : base + PLANE * k + RUN_PAD, :].astype(bf16))
            else:
                rows.append(jnp.zeros((RUN_PAD, WAVE), bf16))
        rows.append(jnp.zeros((16, WAVE), bf16))
        result = jnp.dot(block, jnp.concatenate(rows, axis=0), preferred_element_type=f32)
        for k in kept:
            at = base + PLANE * k
            target[at : at + RUN_PAD, :] += result[RUN_PAD * k : RUN_PAD * (k + 1)]

    def add_layer(cz, source, target, **which):
        for cy in range(CY):
            base = LAYER * cz + 4 * LINE * cy
            add_pair(pairs[CY * cz + cy], base, source, target, **which)

    w32[...] = w_ref[...].astype(f32)
    start[OWN:GRID, :] = jnp.zeros((FACE_PAD, WAVE), f32)
    section[OWN:GRID, :] = jnp.zeros((FACE_PAD, WAVE), f32)

    def gather_layer(cz, carry):
        cleared = pl.ds(pl.multiple_of(TOTAL // CZ * cz, 8), TOTAL // CZ)
        for n in range(2):
            total[n, cleared, :] = jnp.zeros((TOTAL // CZ, WAVE), f32)
        for k in range(4):
            for q in range(COL):
                cy = min(q // 4, CY - 1)
                for p in range(LINE):
                    cx = min(p // 4, CX - 1)
                    slot = (p - 4 * cx) + 5 * (q - 4 * cy) + 25 * k
                    node = nodes_ref[cz, cy * CX + cx, slot]
                    row = cz * LAYER + k * PLANE + q * LINE + p
                    start[pl.ds(row, 1), :] = w32[pl.ds(node, 1), :]
                    ident[pl.ds(row, 1), :] = jnp.full((1, WAVE), node, jnp.int32)
        return carry

    lax.fori_loop(0, CZ, gather_layer, 0)
    pl.semaphore_wait(barrier, len(greeted))
    send_face(0, start)

    @apart
    def _():
        h32[:, 125:WAVE] = jnp.zeros((125 * CX * PAIRS, WAVE - 125), f32)
        h32[:, 0:125] = h_ref[...].astype(f32)

    def make_pairs(p):
        sides = []
        for cell in range(CX):
            cells = [
                h32[pl.ds(CX * (p + q) + cell, 125, stride=CX * PAIRS), :].astype(bf16)
                for q in range(2)
            ]
            side = jnp.dot(
                e_ref[:, 128 * cell : 128 * cell + 125],
                jnp.concatenate(cells, axis=1),
                preferred_element_type=f32,
            )
            sides.append(side.astype(bf16))
        for q in range(2):
            both = [side[:, 128 * q : 128 * (q + 1)] for side in sides]
            block = jnp.dot(
                jnp.concatenate(both, axis=1), et_ref[...], preferred_element_type=f32
            )
            pairs[p + q] = block.astype(bf16)

    def below(n, field):
        add_layer(CZ - 1, field, total.at[n], used=range(4))

        @apart
        def _():
            back_out[n] = total[n, OWN:GRID, :]
            back_copy(n).start()

    def inner(n, field):
        for cz in range(CZ - 1):
            add_layer(cz, field, total.at[n])

    def above(n, field):
        take_face(n, field)
        add_layer(CZ - 1, field, total.at[n], used=(4,), kept=range(4))

    def shared(n, field):
        for cy in range(CY):
            at = 4 * LINE * cy
            rows = jnp.concatenate(
                [
                    jnp.zeros((4 * RUN_PAD, WAVE), bf16),
                    field[at : at + RUN_PAD, :].astype(bf16),
                    jnp.zeros((16, WAVE), bf16),
                ],
                axis=0,
            )
            result = jnp.dot(corner[cy], rows, preferred_element_type=f32)
            total[n, at : at + RUN_PAD, :] += result

    def take_back(n):
        back_copy(n).wait_recv()

        @apart
        def _():
            total[n, 0:FACE_PAD, :] += back_in[n]

    def to_section(lo, hi):
        value = (total[0, lo:hi, :] - filter_center * start[lo:hi, :]) * (1.0 / filter_half)
        section[lo:hi, :] = value.astype(bf16).astype(f32)

    def to_filtered(lo, hi):
        value = (total[1, lo:hi, :] - filter_center * section[lo:hi, :]) * (2.0 / filter_half)
        value = (value - start[lo:hi, :]).astype(bf16)
        compact[lo:hi, :] = value
        start[lo:hi, :] = value.astype(f32)

    make_pairs(PAIRS - 4)
    make_pairs(PAIRS - 2)
    corner_copy.start()
    below(0, start)
    for p in range(0, PAIRS - 4, 2):
        make_pairs(p)
    inner(0, start)
    corner_copy.wait_recv()
    shared(0, start)
    take_back(0)

    @apart
    def _():
        to_section(0, FACE_PAD)
        send_face(1, section)

    above(0, start)
    apart(lambda: to_section(FACE_PAD, OWN))
    below(1, section)
    inner(1, section)
    shared(1, section)
    above(1, section)
    take_back(1)

    @apart
    def _():
        to_filtered(0, OWN)
        send_face(2, start)

    x_rows = (pl.ds(0, EARLY), pl.ds(EARLY, FACE_PAD))
    y_rows = (pl.ds(0, EARLY), pl.ds(EARLY, ACROSS - EARLY))

    def x_copy(j, part):
        return pltpu.make_async_remote_copy(
            src_ref=slabs.at[j, x_rows[part]],
            dst_ref=waves.at[x, x_rows[part]],
            send_sem=x_s.at[part, j],
            recv_sem=x_r.at[part, x],
            device_id=along_x(j),
            device_id_type=MESH,
        )

    def x_arrival(xx, part):
        return pltpu.make_async_remote_copy(
            src_ref=slabs.at[0, x_rows[part]],
            dst_ref=waves.at[xx, x_rows[part]],
            send_sem=x_s.at[part, 0],
            recv_sem=x_r.at[part, xx],
            device_id=along_x(xx),
            device_id_type=MESH,
        )

    def y_copy(xx, part):
        return pltpu.make_async_remote_copy(
            src_ref=waves.at[xx, y_rows[part]],
            dst_ref=waves.at[NX + xx, y_rows[part]],
            send_sem=y_s.at[part, xx],
            recv_sem=y_r.at[part, xx],
            device_id=across,
            device_id_type=MESH,
        )

    def fill_slab(j, part):
        lo, hi = (0, EARLY) if part == 0 else (EARLY, SLAB)
        value = start[LAYER * j + lo : LAYER * j + hi, :].astype(bf16)
        slabs[j, lo:hi, :] = value

        @pl.when(x == j)
        def _():
            waves[j, lo:hi, :] = value
            y_copy(j, part).start()

    def send_slabs(layers, part):
        for j in layers:
            fill_slab(j, part)
        for off in (1, 3, 2):
            jj = lax.rem(x + off, NX)
            wanted = jj == layers[0]
            for j in layers[1:]:
                wanted = jnp.logical_or(wanted, jj == j)

            @pl.when(wanted)
            def _():
                x_copy(jj, part).start()

    send_slabs((0, 1, 2, 3), 0)
    send_slabs((0, 1, 2), 1)

    compact[OWN:SORTED, :] = jnp.zeros((SORTED - OWN, WAVE), bf16)
    ident[OWN:SORTED, :] = jnp.full((SORTED - OWN, WAVE), -1, jnp.int32)
    for t in range(SORTED // WAVE):
        order[:, WAVE * t : WAVE * (t + 1)] = ident[WAVE * t : WAVE * (t + 1), :].T[:8]

    def restore(lo, hi):
        rows = lax.broadcasted_iota(jnp.int32, (hi - lo, 256), 0) + lo
        value = jnp.zeros((hi - lo, WAVE), f32)
        for t in range(SORTED // 256):
            here = jnp.broadcast_to(order[0:1, 256 * t : 256 * (t + 1)], (hi - lo, 256))
            hit = jnp.where(rows == here, 1.0, 0.0).astype(bf16)
            value += jnp.dot(hit, compact[256 * t : 256 * (t + 1), :], preferred_element_type=f32)
        restored[lo:hi, :] = value.astype(bf16)

    def out_copy():
        return pltpu.make_async_copy(restored, filtered_ref, out_s)

    own_rows = lax.broadcasted_iota(jnp.int32, (SLAB, WAVE), 0) < LAYER

    def take_piece(xx):
        @apart
        def _():
            piece[...] = waves[xx].astype(f32)

        def clear(i, carry):
            rows = pl.ds(pl.multiple_of(112 * i, 8), 112)
            image[rows, :] = jnp.zeros((112, WAVE), f32)
            return carry

        lax.fori_loop(0, (SLAB + 16) // 112, clear, 0)

        for cy in range(CY):
            add_pair(pairs[CY * x + cy], 4 * LINE * cy, piece, image)

        @apart
        def _():
            at = pl.multiple_of(2 * WAVE * xx, 2 * WAVE)
            right[:, pl.ds(at, WAVE)] = jnp.where(own_rows, piece[...], 0.0).astype(bf16)
            right[:, pl.ds(at + WAVE, WAVE)] = image[0:SLAB, :].astype(bf16)
            edge_out[xx] = image[LAYER : LAYER + FACE_PAD, :].astype(bf16)

    def pass_on(off, part):
        xx = lax.rem(x + off, NX)
        x_arrival(xx, part).wait_recv()
        y_copy(xx, part).start()

    restore(0, 640)
    take_face(2, start)
    send_slabs((NX - 1,), 1)
    pass_on(1, 0)
    pass_on(3, 0)
    take_piece(x)
    pass_on(1, 1)
    pass_on(2, 0)
    take_piece(lax.rem(x + 1, NX))
    pass_on(3, 1)
    take_piece(lax.rem(x + 3, NX))
    pass_on(2, 1)
    take_piece(lax.rem(x + 2, NX))

    edge_copy = pltpu.make_async_remote_copy(
        src_ref=edge_out,
        dst_ref=edge_in,
        send_sem=edge_s,
        recv_sem=edge_r,
        device_id=next_layer,
        device_id_type=MESH,
    )
    edge_copy.start()

    def complete_image():
        edge_copy.wait_recv()
        last = lax.broadcasted_iota(jnp.int32, (16, WAVE), 0) < LAYER - EARLY
        for xx in range(NX):
            at = 2 * WAVE * xx + WAVE
            value = right[0:FACE_PAD, at : at + WAVE].astype(f32) + edge_in[xx].astype(f32)
            right[0:FACE_PAD, at : at + WAVE] = value.astype(bf16)
            value = right[EARLY:ACROSS, at : at + WAVE].astype(f32)
            right[EARLY:ACROSS, at : at + WAVE] = jnp.where(last, value, 0.0).astype(bf16)

    keep = pl.multiple_of(64 * core, 64)
    give = pl.multiple_of(64 * (1 - core), 64)

    def core_copy(t):
        return pltpu.make_async_remote_copy(
            src_ref=gram.at[t, pl.ds(give, 64)],
            dst_ref=from_core.at[t],
            send_sem=core_s.at[t],
            recv_sem=core_r.at[t],
            device_id=mate,
            device_id_type=MESH,
        )

    def block_of(xx):
        return pl.ds(pl.multiple_of(2 * WAVE * xx, 2 * WAVE), 2 * WAVE)

    def red_copy(t, xx):
        return pltpu.make_async_remote_copy(
            src_ref=half.at[t, :, block_of(xx)],
            dst_ref=from_x.at[t, x],
            send_sem=red_s.at[t, xx],
            recv_sem=red_r.at[t, x],
            device_id=along_x(xx),
            device_id_type=MESH,
        )

    def red_arrival(t, xx):
        return pltpu.make_async_remote_copy(
            src_ref=half.at[t, :, block_of(xx)],
            dst_ref=from_x.at[t, xx],
            send_sem=red_s.at[t, xx],
            recv_sem=red_r.at[t, xx],
            device_id=along_x(xx),
            device_id_type=MESH,
        )

    def target_chip(t):
        band_side = jnp.where(t < NX, yh, 1 - yh)
        return 2 * lax.rem(t, NX) + band_side

    def fin_copy(t):
        return pltpu.make_async_remote_copy(
            src_ref=quarter.at[t],
            dst_ref=final.at[chip],
            send_sem=fin_s.at[t],
            recv_sem=fin_r.at[chip],
            device_id=other_chip(target_chip(t)),
            device_id_type=MESH,
        )

    def fin_arrival(cc):
        return pltpu.make_async_remote_copy(
            src_ref=quarter.at[0],
            dst_ref=final.at[cc],
            send_sem=fin_s.at[0],
            recv_sem=fin_r.at[cc],
            device_id=other_chip(cc),
            device_id_type=MESH,
        )

    def multiply(t, rows):
        gram[t] = lax.dot_general(
            waves[t, 0:rows, :],
            right[0:rows, :],
            (((0,), (0,)), ((), ())),
            preferred_element_type=f32,
        ).astype(bf16)
        core_copy(t).start()

    def sum_core(t):
        core_copy(t).wait_recv()
        value = gram[t, pl.ds(keep, 64), :].astype(f32) + from_core[t].astype(f32)
        half[t] = value.astype(bf16)
        for off in range(1, NX):
            red_copy(t, lax.rem(x + off, NX)).start()

    def sum_x(t):
        value = half[t, :, block_of(x)].astype(f32)
        for off in range(1, NX):
            xx = lax.rem(x + off, NX)
            red_arrival(t, xx).wait_recv()
            value += from_x[t, xx].astype(f32)
        quarter[t] = value.astype(bf16)
        away = target_chip(t) != chip

        @pl.when(away)
        def _():
            fin_copy(t).start()

        @pl.when(jnp.logical_not(away))
        def _():
            final[chip] = quarter[t]

    def own_round(t, carry):
        multiply(t, SLAB)

        @pl.when(t >= 1)
        def _():
            sum_core(t - 1)

        return carry

    lax.fori_loop(0, NX, own_round, 0)
    sum_core(NX - 1)
    for lo, hi in ((640, 1280), (1280, 1920), (1920, OWN)):
        restore(lo, hi)
    out_copy().start()
    apart(complete_image)

    def arrival_order(i):
        off = jnp.where(i == 2, 3, jnp.where(i == 3, 2, i))
        return NX + lax.rem(x + off, NX)

    def other_round(i, carry):
        t = arrival_order(i)
        for part in range(2):
            y_copy(t - NX, part).wait_recv()
        multiply(t, ACROSS)

        @pl.when(i >= 1)
        def _():
            sum_core(arrival_order(i - 1))

        sum_x(i)
        return carry

    lax.fori_loop(0, NX, other_round, 0)
    sum_core(arrival_order(NX - 1))

    def last_round(i, carry):
        sum_x(arrival_order(i))
        return carry

    lax.fori_loop(0, NX, last_round, 0)

    for cc in range(8):

        @pl.when(chip != cc)
        def _():
            fin_arrival(cc).wait_recv()

    result = final[0].astype(f32)
    for cc in range(1, 8):
        result += final[cc].astype(f32)
    sums_ref[...] = result

    for n in range(3):
        face_copy(n).wait_send()
    for n in range(2):
        back_copy(n).wait_send()
    corner_copy.wait_send()
    edge_copy.wait_send()
    for part in range(2):
        for j in range(NX):

            @pl.when(x != j)
            def _():
                x_copy(j, part).wait_send()

            y_copy(j, part).wait_send()

    def drain(t, carry):
        core_copy(t).wait_send()
        for off in range(1, NX):
            red_copy(t, lax.rem(x + off, NX)).wait_send()

        @pl.when(target_chip(t) != chip)
        def _():
            fin_copy(t).wait_send()

        return carry

    lax.fori_loop(0, 2 * NX, drain, 0)
    out_copy().wait()


def shards(wavefunctions, cell_hamiltonian, cell_nodes, face_nodes):
    e = expansion()
    expand = jnp.asarray(e, bf16)
    expand_t = jnp.asarray(np.pad(e.T, ((0, 0), (0, 256 - PAIR))), bf16)
    vmem = pl.BlockSpec(memory_space=pltpu.VMEM)
    dma = pltpu.SemaphoreType.DMA
    by_row = cell_hamiltonian.transpose(1, 0, 2).reshape(125 * CX * PAIRS, 125)
    filtered, sums = pl.pallas_call(
        kernel,
        out_shape=(
            jax.ShapeDtypeStruct((OWN, WAVE), bf16),
            jax.ShapeDtypeStruct((64, 2 * WAVE), f32),
        ),
        in_specs=[vmem, vmem, pl.BlockSpec(memory_space=pltpu.SMEM), vmem, vmem],
        out_specs=(pl.BlockSpec(memory_space=pl.ANY), vmem),
        scratch_shapes=[
            pltpu.VMEM((OWN, WAVE), f32),
            pltpu.VMEM((125 * CX * PAIRS, WAVE), f32),
            pltpu.VMEM((SORTED, WAVE), jnp.int32),
            pltpu.VMEM((8, SORTED), jnp.int32),
            pltpu.VMEM((GRID, WAVE), f32),
            pltpu.VMEM((GRID, WAVE), f32),
            pltpu.VMEM((2, TOTAL, WAVE), f32),
            pltpu.VMEM((PAIRS, PAIR, 256), bf16),
            pltpu.VMEM((3, FACE_PAD, WAVE), bf16),
            pltpu.VMEM((3, FACE_PAD, WAVE), bf16),
            pltpu.VMEM((2, FACE_PAD, WAVE), f32),
            pltpu.VMEM((2, FACE_PAD, WAVE), f32),
            pltpu.VMEM((CY, RUN_PAD, 256), bf16),
            pltpu.VMEM((NX, FACE_PAD, WAVE), bf16),
            pltpu.VMEM((NX, FACE_PAD, WAVE), bf16),
            pltpu.VMEM((NX, SLAB, WAVE), bf16),
            pltpu.VMEM((2 * NX, SLAB, WAVE), bf16),
            pltpu.VMEM((SORTED, WAVE), bf16),
            pltpu.VMEM((OWN, WAVE), bf16),
            pltpu.VMEM((SLAB, WAVE), f32),
            pltpu.VMEM((SLAB + 16, WAVE), f32),
            pltpu.VMEM((SLAB, 2 * NX * WAVE), bf16),
            pltpu.VMEM((2 * NX, WAVE, 2 * NX * WAVE), bf16),
            pltpu.VMEM((2 * NX, 64, 2 * NX * WAVE), bf16),
            pltpu.VMEM((2 * NX, 64, 2 * NX * WAVE), bf16),
            pltpu.VMEM((2 * NX, NX, 64, 2 * WAVE), bf16),
            pltpu.VMEM((2 * NX, 64, 2 * WAVE), bf16),
            pltpu.VMEM((8, 64, 2 * WAVE), bf16),
            dma((3,)),
            dma((3,)),
            dma((2,)),
            dma((2,)),
            dma,
            dma,
            dma,
            dma,
            dma((2, NX)),
            dma((2, NX)),
            dma((2, NX)),
            dma((2, NX)),
            dma((2 * NX,)),
            dma((2 * NX,)),
            dma((2 * NX, NX)),
            dma((2 * NX, NX)),
            dma((2 * NX,)),
            dma((8,)),
            dma,
        ],
        compiler_params=pltpu.CompilerParams(
            collective_id=0, has_side_effects=True, vmem_limit_bytes=48 << 20
        ),
        name="chebyshev_filter",
    )(wavefunctions, by_row, cell_nodes.reshape(CZ, CX * CY, 125), expand, expand_t)
    nodes = lax.axis_size("dom") * OWN
    return filtered, sums[:, :WAVE] / nodes, sums[:, WAVE:] / nodes


def solution(mesh):
    placed = (P("dom", "band"), P("dom", None, None), P("dom", None), P("dom"))
    return jax.shard_map(
        shards,
        mesh=mesh,
        in_specs=placed,
        out_specs=(P("dom", "band"), P("dom", "band"), P("dom", "band")),
        check_vma=False,
    )
```

time: 69.8 us -> 58 us (0.83)
  the two profiles are of different devices: /device:TPU:112 before, /device:TPU:12 now
where the time goes in v1:
time: 58 us; the launch traced here: 57.7 us
  Pallas kernels  50.8 us (88%)
  local copies, waits for them, and re-layouts  5.63 us (10%)
  between operations  0.65 us (1%)
  other arithmetic  0.63 us (1%)
    pallas_call x1, Pallas kernels, shards(): pl.pallas_call(kernel, out_shape=(jax.ShapeDtypeStruct((OWN, WAVE), bf16)...  50.8 us
    unnamed x11, local copies, waits for them, and re-layouts  5.63 us

profile of v1, /device:TPU:12, one launch (start us, length us, event | category | flops | bytes accessed | tf_op | source)
XLA Modules:
  0.0 57.7 jit_solution(18232595759873665291)
XLA Ops:
  0.6 0.0 copy-start
  0.6 1.2 %copy-done = bf16[32,125,125]{2,0,1:T(8,128)(2,1)S(1)} copy-done((bf16[32,125,125]{2,0,1:T(8,128)(2,1)S(1)}, bf16[32,125,125]{2,0,1:T(8,128)(2,1)}, u32[]{:S(2)}) %copy-start) | copy-done | bytes 1000024
  1.8 0.0 copy-start.1
  1.9 1.1 %copy-done.1 = bf16[2448,128]{1,0:T(8,128)(2,1)S(1)} copy-done((bf16[2448,128]{1,0:T(8,128)(2,1)S(1)}, bf16[2448,128]{1,0:T(8,128)(2,1)}, u32[]{:S(2)}) %copy-start.1) | copy-done | bytes 626712
  2.9 0.0 copy-start.2
  2.9 0.9 %copy-done.2 = bf16[256,256]{1,0:T(8,128)(2,1)S(1)} copy-done((bf16[256,256]{1,0:T(8,128)(2,1)S(1)}, bf16[256,256]{1,0:T(8,128)(2,1)}, u32[]{:S(2)}) %copy-start.2) | copy-done | bytes 131096
  3.8 0.0 copy-start.3
  3.8 0.9 %copy-done.3 = bf16[240,256]{1,0:T(8,128)(2,1)S(1)} copy-done((bf16[240,256]{1,0:T(8,128)(2,1)S(1)}, bf16[240,256]{1,0:T(8,128)(2,1)}, u32[]{:S(2)}) %copy-start.3) | copy-done | bytes 122904
  4.7 0.0 copy-start.4
  4.7 0.7 %copy-done.4 = s32[32,125]{1,0:T(8,128)S(1)} copy-done((s32[32,125]{1,0:T(8,128)S(1)}, s32[32,125]{1,0:T(8,128)}, u32[]{:S(2)}) %copy-start.4) | copy-done | bytes 16024
  5.5 50.8 %chebyshev_filter.1 = (bf16[2448,128]{1,0:T(8,128)(2,1)S(1)}, f32[64,256]{1,0:T(8,128)S(1)}) custom-call(bf16[2448,128]{1,0:T(8,128)(2,1)S(1)} %copy-done.1, bf16[4000,125]{1,0:T(8,128)(2,1)S(1)} %bitcast.4, s32[4,8,125]{2,1,0:T(8,128)S(1)} %bitcast.5, bf16[240,256]{1,0:T(8,128)(2,1)S(1)} %copy-done.3, bf16[256,256]{1,0:T(8,128)(2,1)S(1)} %copy-done.2), custom_call_target="tpu_custom_call" | custom-call | tf_op jit(solution)/shard_map/chebyshev_filter/pallas_call | solution.py:647
  56.3 0.6 %slice_multiply_fusion = (f32[64,128]{1,0:T(8,128)}, f32[64,128]{1,0:T(8,128)}) fusion(f32[64,256]{1,0:T(8,128)S(1)} %get-tuple-element.6), kind=kLoop, calls=%fused_computation | loop fusion | flops 16384 | bytes 131072 | tf_op jit(solution)/shard_map/div | solution.py:710
  56.9 0.8 %copy.9 = bf16[2448,128]{1,0:T(8,128)(2,1)} copy(bf16[2448,128]{1,0:T(8,128)(2,1)S(1)} %get-tuple-element.12) | data formatting | bytes 1253376
Async XLA Ops:
  0.6 1.2 %copy-start = (bf16[32,125,125]{2,0,1:T(8,128)(2,1)S(1)}, bf16[32,125,125]{2,0,1:T(8,128)(2,1)}, u32[]{:S(2)}) copy-start(bf16[32,125,125]{2,0,1:T(8,128)(2,1)} %param.7) | copy-start | bytes 3000004
  1.8 1.1 %copy-start.1 = (bf16[2448,128]{1,0:T(8,128)(2,1)S(1)}, bf16[2448,128]{1,0:T(8,128)(2,1)}, u32[]{:S(2)}) copy-start(bf16[2448,128]{1,0:T(8,128)(2,1)} %w_ref.1) | copy-start | bytes 1880068
  2.9 0.9 %copy-start.2 = (bf16[256,256]{1,0:T(8,128)(2,1)S(1)}, bf16[256,256]{1,0:T(8,128)(2,1)}, u32[]{:S(2)}) copy-start(bf16[256,256]{1,0:T(8,128)(2,1)} %constant.9.clone.et_ref) | copy-start | bytes 393220
  3.8 0.9 %copy-start.3 = (bf16[240,256]{1,0:T(8,128)(2,1)S(1)}, bf16[240,256]{1,0:T(8,128)(2,1)}, u32[]{:S(2)}) copy-start(bf16[240,256]{1,0:T(8,128)(2,1)} %constant.8.clone.e_ref) | copy-start | bytes 368644
  4.7 0.7 %copy-start.4 = (s32[32,125]{1,0:T(8,128)S(1)}, s32[32,125]{1,0:T(8,128)}, u32[]{:S(2)}) copy-start(s32[32,125]{1,0:T(8,128)} %param.8) | copy-start | bytes 48004

commit v2 on v1

--- a/solution.py
+++ b/solution.py
@@ -47,13 +47,18 @@
 
 
 def kernel(
+    w_hbm,
+    h_hbm,
+    nodes_hbm,
+    e_hbm,
+    et_hbm,
+    filtered_ref,
+    sums_ref,
     w_ref,
     h_ref,
     nodes_ref,
     e_ref,
     et_ref,
-    filtered_ref,
-    sums_ref,
     w32,
     h32,
     ident,
@@ -101,6 +106,7 @@
     fin_s,
     fin_r,
     out_s,
+    in_s,
 ):
     d = lax.axis_index("dom")
     b = lax.axis_index("band")
@@ -123,6 +129,21 @@
     def other_chip(cc):
         return (2 * cc + core, b)
 
+    loads = [
+        pltpu.make_async_copy(source, target, in_s.at[n])
+        for n, (source, target) in enumerate(
+            (
+                (nodes_hbm, nodes_ref),
+                (w_hbm, w_ref),
+                (h_hbm, h_ref),
+                (e_hbm, e_ref),
+                (et_hbm, et_ref),
+            )
+        )
+    ]
+    for load in loads:
+        load.start()
+
     barrier = pltpu.get_barrier_semaphore()
     greeted = [(prev, b), (succ, b), mate, across, next_layer]
     greeted += [along_x(lax.rem(x + off, NX)) for off in range(1, NX)]
@@ -197,6 +218,8 @@
             base = LAYER * cz + 4 * LINE * cy
             add_pair(pairs[CY * cz + cy], base, source, target, **which)
 
+    loads[0].wait()
+    loads[1].wait()
     w32[...] = w_ref[...].astype(f32)
     start[OWN:GRID, :] = jnp.zeros((FACE_PAD, WAVE), f32)
     section[OWN:GRID, :] = jnp.zeros((FACE_PAD, WAVE), f32)
@@ -214,10 +237,11 @@
                     node = nodes_ref[cz, cy * CX + cx, slot]
                     row = cz * LAYER + k * PLANE + q * LINE + p
                     start[pl.ds(row, 1), :] = w32[pl.ds(node, 1), :]
-                    ident[pl.ds(row, 1), :] = jnp.full((1, WAVE), node, jnp.int32)
         return carry
 
     lax.fori_loop(0, CZ, gather_layer, 0)
+    for load in loads[2:]:
+        load.wait()
     pl.semaphore_wait(barrier, len(greeted))
     send_face(0, start)
 
@@ -315,6 +339,20 @@
     inner(1, section)
     shared(1, section)
     above(1, section)
+
+    def number_layer(cz, carry):
+        for k in range(4):
+            for q in range(COL):
+                cy = min(q // 4, CY - 1)
+                for p in range(LINE):
+                    cx = min(p // 4, CX - 1)
+                    slot = (p - 4 * cx) + 5 * (q - 4 * cy) + 25 * k
+                    node = nodes_ref[cz, cy * CX + cx, slot]
+                    row = cz * LAYER + k * PLANE + q * LINE + p
+                    ident[pl.ds(row, 1), :] = jnp.full((1, WAVE), node, jnp.int32)
+        return carry
+
+    lax.fori_loop(0, CZ, number_layer, 0)
     take_back(1)
 
     @apart
@@ -421,11 +459,22 @@
             right[:, pl.ds(at, WAVE)] = jnp.where(own_rows, piece[...], 0.0).astype(bf16)
             right[:, pl.ds(at + WAVE, WAVE)] = image[0:SLAB, :].astype(bf16)
             edge_out[xx] = image[LAYER : LAYER + FACE_PAD, :].astype(bf16)
+            edge_copy(xx).start()
 
     def pass_on(off, part):
         xx = lax.rem(x + off, NX)
         x_arrival(xx, part).wait_recv()
         y_copy(xx, part).start()
+
+    def edge_copy(xx):
+        return pltpu.make_async_remote_copy(
+            src_ref=edge_out.at[xx],
+            dst_ref=edge_in.at[xx],
+            send_sem=edge_s.at[xx],
+            recv_sem=edge_r.at[xx],
+            device_id=next_layer,
+            device_id_type=MESH,
+        )
 
     restore(0, 640)
     take_face(2, start)
@@ -433,26 +482,17 @@
     pass_on(1, 0)
     pass_on(3, 0)
     take_piece(x)
+    pass_on(2, 0)
     pass_on(1, 1)
-    pass_on(2, 0)
     take_piece(lax.rem(x + 1, NX))
     pass_on(3, 1)
     take_piece(lax.rem(x + 3, NX))
     pass_on(2, 1)
     take_piece(lax.rem(x + 2, NX))
 
-    edge_copy = pltpu.make_async_remote_copy(
-        src_ref=edge_out,
-        dst_ref=edge_in,
-        send_sem=edge_s,
-        recv_sem=edge_r,
-        device_id=next_layer,
-        device_id_type=MESH,
-    )
-    edge_copy.start()
-
     def complete_image():
-        edge_copy.wait_recv()
+        for xx in range(NX):
+            edge_copy(xx).wait_recv()
         last = lax.broadcasted_iota(jnp.int32, (16, WAVE), 0) < LAYER - EARLY
         for xx in range(NX):
             at = 2 * WAVE * xx + WAVE
@@ -605,14 +645,15 @@
     result = final[0].astype(f32)
     for cc in range(1, 8):
         result += final[cc].astype(f32)
-    sums_ref[...] = result
+    sums_ref[...] = result * (1.0 / (n_dom * OWN))
 
     for n in range(3):
         face_copy(n).wait_send()
     for n in range(2):
         back_copy(n).wait_send()
     corner_copy.wait_send()
-    edge_copy.wait_send()
+    for xx in range(NX):
+        edge_copy(xx).wait_send()
     for part in range(2):
         for j in range(NX):
 
@@ -635,6 +676,26 @@
 
     lax.fori_loop(0, 2 * NX, drain, 0)
     out_copy().wait()
+
+
+def finish(filtered_ref, sums_ref, out_ref, corr_ref, proj_ref, sums, held, sem):
+    whole = pltpu.make_async_copy(filtered_ref, held, sem.at[0])
+    whole.start()
+    load = pltpu.make_async_copy(sums_ref, sums, sem.at[1])
+    load.start()
+    load.wait()
+    stores = [
+        pltpu.make_async_copy(sums.at[:, pl.ds(WAVE * n, WAVE)], target, sem.at[2 + n])
+        for n, target in enumerate((corr_ref, proj_ref))
+    ]
+    for store in stores:
+        store.start()
+    whole.wait()
+    back = pltpu.make_async_copy(held, out_ref, sem.at[4])
+    back.start()
+    for store in stores:
+        store.wait()
+    back.wait()
 
 
 def shards(wavefunctions, cell_hamiltonian, cell_nodes, face_nodes):
@@ -650,9 +711,14 @@
             jax.ShapeDtypeStruct((OWN, WAVE), bf16),
             jax.ShapeDtypeStruct((64, 2 * WAVE), f32),
         ),
-        in_specs=[vmem, vmem, pl.BlockSpec(memory_space=pltpu.SMEM), vmem, vmem],
+        in_specs=[pl.BlockSpec(memory_space=pltpu.HBM)] * 5,
         out_specs=(pl.BlockSpec(memory_space=pl.ANY), vmem),
         scratch_shapes=[
+            pltpu.VMEM((OWN, WAVE), bf16),
+            pltpu.VMEM((125 * CX * PAIRS, 125), bf16),
+            pltpu.SMEM((CZ, CX * CY, 125), jnp.int32),
+            pltpu.VMEM((PAIR, 256), bf16),
+            pltpu.VMEM((256, 256), bf16),
             pltpu.VMEM((OWN, WAVE), f32),
             pltpu.VMEM((125 * CX * PAIRS, WAVE), f32),
             pltpu.VMEM((SORTED, WAVE), jnp.int32),
@@ -687,8 +753,8 @@
             dma((2,)),
             dma,
             dma,
-            dma,
-            dma,
+            dma((NX,)),
+            dma((NX,)),
             dma((2, NX)),
             dma((2, NX)),
             dma((2, NX)),
@@ -700,14 +766,31 @@
             dma((2 * NX,)),
             dma((8,)),
             dma,
+            dma((5,)),
         ],
         compiler_params=pltpu.CompilerParams(
-            collective_id=0, has_side_effects=True, vmem_limit_bytes=48 << 20
+            collective_id=0, has_side_effects=True, vmem_limit_bytes=63 << 20
         ),
         name="chebyshev_filter",
     )(wavefunctions, by_row, cell_nodes.reshape(CZ, CX * CY, 125), expand, expand_t)
-    nodes = lax.axis_size("dom") * OWN
-    return filtered, sums[:, :WAVE] / nodes, sums[:, WAVE:] / nodes
+    hbm = pl.BlockSpec(memory_space=pltpu.HBM)
+    return pl.pallas_call(
+        finish,
+        out_shape=(
+            jax.ShapeDtypeStruct((OWN, WAVE), bf16),
+            jax.ShapeDtypeStruct((64, WAVE), f32),
+            jax.ShapeDtypeStruct((64, WAVE), f32),
+        ),
+        in_specs=[hbm, hbm],
+        out_specs=(hbm, hbm, hbm),
+        scratch_shapes=[
+            pltpu.VMEM((64, 2 * WAVE), f32),
+            pltpu.VMEM((OWN, WAVE), bf16),
+            dma((5,)),
+        ],
+        compiler_params=pltpu.CompilerParams(vmem_limit_bytes=63 << 20),
+        name="finish",
+    )(filtered, sums)
 
 
 def solution(mesh):

time: 58 us -> 53.8 us (0.928)
  local copies, waits for them, and re-layouts: 5.63 us -> 0 us
  Pallas kernels: 50.8 us -> 53 us
  other arithmetic: 0.63 us -> 0 us
    unnamed x11 -> x0, local copies, waits for them, and re-layouts: 5.63 us -> none
    pallas_call x0 -> x1, Pallas kernels: none -> 1.95 us  [shards(): pl.pallas_call(finish, out_shape=(jax.ShapeDtypeStruct((OWN, WAVE), bf16)...]
    div x1 -> x0, other arithmetic: 0.63 us -> none  [shards(): return (filtered, sums[:, :WAVE] / nodes, sums[:, WAVE:] / nodes)]
where the time goes in v2:
time: 53.8 us; the launch traced here: 53.6 us
  Pallas kernels  53 us (99%)
  between operations  0.64 us (1%)
    pallas_call x1, Pallas kernels, shards(): pl.pallas_call(kernel, out_shape=(jax.ShapeDtypeStruct((OWN, WAVE), bf16)...  51 us
    pallas_call x1, Pallas kernels, shards(): pl.pallas_call(finish, out_shape=(jax.ShapeDtypeStruct((OWN, WAVE), bf16)...  1.95 us

profile of v2, /device:TPU:12, one launch (start us, length us, event | category | flops | bytes accessed | tf_op | source)
XLA Modules:
  0.0 53.6 jit_solution(16104205171652119061)
XLA Ops:
  0.6 51.0 %chebyshev_filter.1 = (bf16[2448,128]{1,0:T(8,128)(2,1)}, f32[64,256]{1,0:T(8,128)}) custom-call(bf16[2448,128]{1,0:T(8,128)(2,1)} %w_hbm.1, bf16[4000,125]{1,0:T(8,128)(2,1)} %bitcast.4, s32[4,8,125]{2,1,0:T(8,128)} %bitcast.5, bf16[240,256]{1,0:T(8,128)(2,1)} %constant.4.clone.e_hbm, bf16[256,256]{1,0:T(8,128)(2,1)} %constant.5.clone.et_hbm), custom_call_target="tpu_custom_call" | custom-call | tf_op jit(solution)/shard_map/chebyshev_filter/pallas_call | solution.py:708
  51.7 1.9 %finish.1 = (bf16[2448,128]{1,0:T(8,128)(2,1)}, f32[64,128]{1,0:T(8,128)}, f32[64,128]{1,0:T(8,128)}) custom-call(bf16[2448,128]{1,0:T(8,128)(2,1)} %get-tuple-element.5.filtered_ref, f32[64,256]{1,0:T(8,128)} %get-tuple-element.6.sums_ref), custom_call_target="tpu_custom_call" | custom-call | tf_op jit(solution)/shard_map/finish/pallas_call | solution.py:777

commit v3 on v2

--- a/solution.py
+++ b/solution.py
@@ -22,6 +22,9 @@
 SLAB = 768
 EARLY = SLAB - FACE_PAD
 ACROSS = EARLY + 16
+HELD = ACROSS + FACE_PAD
+READY = 3 * LAYER
+PITCH = CX * PAIRS + 1
 NX = 4
 WAVE = 128
 SORTED = 2560
@@ -85,6 +88,7 @@
     from_core,
     half,
     from_x,
+    from_z,
     quarter,
     final,
     face_s,
@@ -103,6 +107,8 @@
     core_r,
     red_s,
     red_r,
+    z_s,
+    z_r,
     fin_s,
     fin_r,
     out_s,
@@ -247,14 +253,22 @@
 
     @apart
     def _():
-        h32[:, 125:WAVE] = jnp.zeros((125 * CX * PAIRS, WAVE - 125), f32)
-        h32[:, 0:125] = h_ref[...].astype(f32)
+        def fill(i, carry):
+            for u in range(5):
+                row = 5 * i + u
+                here = pl.ds(PITCH * row, CX * PAIRS)
+                there = pl.ds(pl.multiple_of(CX * PAIRS * row, CX * PAIRS), CX * PAIRS)
+                h32[here, 125:WAVE] = jnp.zeros((CX * PAIRS, WAVE - 125), f32)
+                h32[here, 0:125] = h_ref[there, :].astype(f32)
+            return carry
+
+        lax.fori_loop(0, 25, fill, 0)
 
     def make_pairs(p):
         sides = []
         for cell in range(CX):
             cells = [
-                h32[pl.ds(CX * (p + q) + cell, 125, stride=CX * PAIRS), :].astype(bf16)
+                h32[pl.ds(CX * (p + q) + cell, 125, stride=PITCH), :].astype(bf16)
                 for q in range(2)
             ]
             side = jnp.dot(
@@ -314,7 +328,6 @@
     def to_filtered(lo, hi):
         value = (total[1, lo:hi, :] - filter_center * section[lo:hi, :]) * (2.0 / filter_half)
         value = (value - start[lo:hi, :]).astype(bf16)
-        compact[lo:hi, :] = value
         start[lo:hi, :] = value.astype(f32)
 
     make_pairs(PAIRS - 4)
@@ -338,6 +351,81 @@
     below(1, section)
     inner(1, section)
     shared(1, section)
+    x_rows = (pl.ds(0, ACROSS), pl.ds(ACROSS, FACE_PAD))
+
+    def x_copy(j, part):
+        return pltpu.make_async_remote_copy(
+            src_ref=slabs.at[j, x_rows[part]],
+            dst_ref=waves.at[x, x_rows[part]],
+            send_sem=x_s.at[part, j],
+            recv_sem=x_r.at[part, x],
+            device_id=along_x(j),
+            device_id_type=MESH,
+        )
+
+    def x_arrival(xx, part):
+        return pltpu.make_async_remote_copy(
+            src_ref=slabs.at[0, x_rows[part]],
+            dst_ref=waves.at[xx, x_rows[part]],
+            send_sem=x_s.at[part, 0],
+            recv_sem=x_r.at[part, xx],
+            device_id=along_x(xx),
+            device_id_type=MESH,
+        )
+
+    def y_copy(xx):
+        return pltpu.make_async_remote_copy(
+            src_ref=waves.at[xx, pl.ds(0, ACROSS)],
+            dst_ref=waves.at[NX + xx, pl.ds(0, ACROSS)],
+            send_sem=y_s.at[xx],
+            recv_sem=y_r.at[xx],
+            device_id=across,
+            device_id_type=MESH,
+        )
+
+    def keep_compact():
+        compact[0:OWN, :] = start[0:OWN, :].astype(bf16)
+
+    def fill_slab(j, part):
+        base = LAYER * j
+        if part == 0:
+            last = lax.broadcasted_iota(jnp.int32, (ACROSS - EARLY, WAVE), 0) < LAYER - EARLY
+            value = jnp.concatenate(
+                [
+                    start[base : base + EARLY, :],
+                    jnp.where(last, start[base + EARLY : base + ACROSS, :], 0.0),
+                ],
+                axis=0,
+            ).astype(bf16)
+            lo, hi = 0, ACROSS
+        else:
+            value = start[base + EARLY : base + SLAB, :].astype(bf16)
+            lo, hi = ACROSS, HELD
+        slabs[j, lo:hi, :] = value
+
+        @pl.when(x == j)
+        def _():
+            waves[j, lo:hi, :] = value
+            if part == 0:
+                y_copy(j).start()
+
+    def send_slabs(layers, part, offs):
+        for off in offs:
+            jj = lax.rem(x + off, NX)
+            wanted = jj == layers[0]
+            for j in layers[1:]:
+                wanted = jnp.logical_or(wanted, jj == j)
+
+            @pl.when(wanted)
+            def _():
+                x_copy(jj, part).start()
+
+    apart(lambda: to_filtered(FACE_PAD, READY))
+    for j, part in ((1, 0), (2, 0), (1, 1)):
+        fill_slab(j, part)
+    send_slabs((1, 2), 0, (1, 3, 2))
+    send_slabs((1,), 1, (1, 3, 2))
+
     above(1, section)
 
     def number_layer(cz, carry):
@@ -357,67 +445,15 @@
 
     @apart
     def _():
-        to_filtered(0, OWN)
+        to_filtered(0, FACE_PAD)
+        to_filtered(READY, OWN)
         send_face(2, start)
 
-    x_rows = (pl.ds(0, EARLY), pl.ds(EARLY, FACE_PAD))
-    y_rows = (pl.ds(0, EARLY), pl.ds(EARLY, ACROSS - EARLY))
-
-    def x_copy(j, part):
-        return pltpu.make_async_remote_copy(
-            src_ref=slabs.at[j, x_rows[part]],
-            dst_ref=waves.at[x, x_rows[part]],
-            send_sem=x_s.at[part, j],
-            recv_sem=x_r.at[part, x],
-            device_id=along_x(j),
-            device_id_type=MESH,
-        )
-
-    def x_arrival(xx, part):
-        return pltpu.make_async_remote_copy(
-            src_ref=slabs.at[0, x_rows[part]],
-            dst_ref=waves.at[xx, x_rows[part]],
-            send_sem=x_s.at[part, 0],
-            recv_sem=x_r.at[part, xx],
-            device_id=along_x(xx),
-            device_id_type=MESH,
-        )
-
-    def y_copy(xx, part):
-        return pltpu.make_async_remote_copy(
-            src_ref=waves.at[xx, y_rows[part]],
-            dst_ref=waves.at[NX + xx, y_rows[part]],
-            send_sem=y_s.at[part, xx],
-            recv_sem=y_r.at[part, xx],
-            device_id=across,
-            device_id_type=MESH,
-        )
-
-    def fill_slab(j, part):
-        lo, hi = (0, EARLY) if part == 0 else (EARLY, SLAB)
-        value = start[LAYER * j + lo : LAYER * j + hi, :].astype(bf16)
-        slabs[j, lo:hi, :] = value
-
-        @pl.when(x == j)
-        def _():
-            waves[j, lo:hi, :] = value
-            y_copy(j, part).start()
-
-    def send_slabs(layers, part):
-        for j in layers:
-            fill_slab(j, part)
-        for off in (1, 3, 2):
-            jj = lax.rem(x + off, NX)
-            wanted = jj == layers[0]
-            for j in layers[1:]:
-                wanted = jnp.logical_or(wanted, jj == j)
-
-            @pl.when(wanted)
-            def _():
-                x_copy(jj, part).start()
-
-    send_slabs((0, 1, 2, 3), 0)
-    send_slabs((0, 1, 2), 1)
+    for j, part in ((0, 0), (3, 0), (0, 1), (2, 1)):
+        fill_slab(j, part)
+    send_slabs((0, 3), 0, (1, 3, 2))
+    send_slabs((0, 2), 1, (1, 3, 2))
+    apart(keep_compact)
 
     compact[OWN:SORTED, :] = jnp.zeros((SORTED - OWN, WAVE), bf16)
     ident[OWN:SORTED, :] = jnp.full((SORTED - OWN, WAVE), -1, jnp.int32)
@@ -441,7 +477,8 @@
     def take_piece(xx):
         @apart
         def _():
-            piece[...] = waves[xx].astype(f32)
+            piece[0:EARLY, :] = waves[xx, 0:EARLY, :].astype(f32)
+            piece[EARLY:SLAB, :] = waves[xx, ACROSS:HELD, :].astype(f32)
 
         def clear(i, carry):
             rows = pl.ds(pl.multiple_of(112 * i, 8), 112)
@@ -464,7 +501,8 @@
     def pass_on(off, part):
         xx = lax.rem(x + off, NX)
         x_arrival(xx, part).wait_recv()
-        y_copy(xx, part).start()
+        if part == 0:
+            y_copy(xx).start()
 
     def edge_copy(xx):
         return pltpu.make_async_remote_copy(
@@ -478,7 +516,8 @@
 
     restore(0, 640)
     take_face(2, start)
-    send_slabs((NX - 1,), 1)
+    fill_slab(NX - 1, 1)
+    send_slabs((NX - 1,), 1, (1, 3, 2))
     pass_on(1, 0)
     pass_on(3, 0)
     take_piece(x)
@@ -561,12 +600,37 @@
             device_id_type=MESH,
         )
 
-    def multiply(t, rows):
+    z = lax.div(chip, 2)
+
+    def z_copy(t):
+        return pltpu.make_async_remote_copy(
+            src_ref=half.at[t],
+            dst_ref=from_z.at[z],
+            send_sem=z_s.at[t],
+            recv_sem=z_r.at[z],
+            device_id=other_chip(2 * t + yl),
+            device_id_type=MESH,
+        )
+
+    def z_arrival(zz):
+        return pltpu.make_async_remote_copy(
+            src_ref=half.at[zz],
+            dst_ref=from_z.at[zz],
+            send_sem=z_s.at[zz],
+            recv_sem=z_r.at[zz],
+            device_id=other_chip(2 * zz + yl),
+            device_id_type=MESH,
+        )
+
+    def multiply(t, own):
+        if own:
+            left = jnp.concatenate([waves[t, 0:EARLY, :], waves[t, ACROSS:HELD, :]], axis=0)
+            factor = right[...]
+        else:
+            left = waves[t, 0:ACROSS, :]
+            factor = right[0:ACROSS, :]
         gram[t] = lax.dot_general(
-            waves[t, 0:rows, :],
-            right[0:rows, :],
-            (((0,), (0,)), ((), ())),
-            preferred_element_type=f32,
+            left, factor, (((0,), (0,)), ((), ())), preferred_element_type=f32
         ).astype(bf16)
         core_copy(t).start()
 
@@ -574,8 +638,19 @@
         core_copy(t).wait_recv()
         value = gram[t, pl.ds(keep, 64), :].astype(f32) + from_core[t].astype(f32)
         half[t] = value.astype(bf16)
+
+    def send_x(t):
         for off in range(1, NX):
             red_copy(t, lax.rem(x + off, NX)).start()
+
+    def sum_z():
+        value = half[z].astype(f32)
+        for off in range(1, CZ):
+            zz = lax.rem(z + off, CZ)
+            z_arrival(zz).wait_recv()
+            value += from_z[zz].astype(f32)
+        half[z] = value.astype(bf16)
+        send_x(z)
 
     def sum_x(t):
         value = half[t, :, block_of(x)].astype(f32)
@@ -595,57 +670,72 @@
             final[chip] = quarter[t]
 
     def own_round(t, carry):
-        multiply(t, SLAB)
-
-        @pl.when(t >= 1)
-        def _():
-            sum_core(t - 1)
-
+        multiply(t, True)
         return carry
 
     lax.fori_loop(0, NX, own_round, 0)
-    sum_core(NX - 1)
-    for lo, hi in ((640, 1280), (1280, 1920), (1920, OWN)):
-        restore(lo, hi)
-    out_copy().start()
+
+    def own_sum(t, carry):
+        sum_core(t)
+
+        @pl.when(t != z)
+        def _():
+            z_copy(t).start()
+
+        return carry
+
+    lax.fori_loop(0, NX, own_sum, 0)
+    restore(640, 1280)
+    restore(1280, 1920)
     apart(complete_image)
 
     def arrival_order(i):
         off = jnp.where(i == 2, 3, jnp.where(i == 3, 2, i))
         return NX + lax.rem(x + off, NX)
 
+    def other_sum(i):
+        sum_core(arrival_order(i))
+        send_x(arrival_order(i))
+
     def other_round(i, carry):
+        @pl.when(i >= 1)
+        def _():
+            other_sum(i - 1)
+
         t = arrival_order(i)
-        for part in range(2):
-            y_copy(t - NX, part).wait_recv()
-        multiply(t, ACROSS)
-
-        @pl.when(i >= 1)
-        def _():
-            sum_core(arrival_order(i - 1))
-
-        sum_x(i)
+        y_copy(t - NX).wait_recv()
+        multiply(t, False)
         return carry
 
     lax.fori_loop(0, NX, other_round, 0)
-    sum_core(arrival_order(NX - 1))
+    other_sum(NX - 1)
+    sum_z()
+    restore(1920, OWN)
+    out_copy().start()
 
     def last_round(i, carry):
         sum_x(arrival_order(i))
         return carry
 
     lax.fori_loop(0, NX, last_round, 0)
-
-    for cc in range(8):
-
-        @pl.when(chip != cc)
-        def _():
-            fin_arrival(cc).wait_recv()
-
-    result = final[0].astype(f32)
-    for cc in range(1, 8):
-        result += final[cc].astype(f32)
-    sums_ref[...] = result * (1.0 / (n_dom * OWN))
+    sum_x(z)
+
+    nodes = n_dom * OWN
+
+    @pl.when(yl == yh)
+    def _():
+        fin_arrival(2 * z + 1 - yl).wait_recv()
+        result = final[2 * z].astype(f32) + final[2 * z + 1].astype(f32)
+        sums_ref[...] = result * (1.0 / nodes)
+
+    @pl.when(yl != yh)
+    def _():
+        for off in range(1, 8):
+            fin_arrival(lax.rem(chip + off, 8)).wait_recv()
+        result = final[0].astype(f32)
+        for cc in range(1, 8):
+            result += final[cc].astype(f32)
+        sums_ref[...] = result * (1.0 / nodes)
 
     for n in range(3):
         face_copy(n).wait_send()
@@ -654,6 +744,8 @@
     corner_copy.wait_send()
     for xx in range(NX):
         edge_copy(xx).wait_send()
+    for j in range(NX):
+        y_copy(j).wait_send()
     for part in range(2):
         for j in range(NX):
 
@@ -661,16 +753,22 @@
             def _():
                 x_copy(j, part).wait_send()
 
-            y_copy(j, part).wait_send()
 
     def drain(t, carry):
         core_copy(t).wait_send()
-        for off in range(1, NX):
-            red_copy(t, lax.rem(x + off, NX)).wait_send()
-
-        @pl.when(target_chip(t) != chip)
-        def _():
-            fin_copy(t).wait_send()
+
+        @pl.when(jnp.logical_or(t >= NX, t == z))
+        def _():
+            for off in range(1, NX):
+                red_copy(t, lax.rem(x + off, NX)).wait_send()
+
+            @pl.when(target_chip(t) != chip)
+            def _():
+                fin_copy(t).wait_send()
+
+        @pl.when(jnp.logical_and(t < NX, t != z))
+        def _():
+            z_copy(t).wait_send()
 
         return carry
 
@@ -679,23 +777,33 @@
 
 
 def finish(filtered_ref, sums_ref, out_ref, corr_ref, proj_ref, sums, held, sem):
-    whole = pltpu.make_async_copy(filtered_ref, held, sem.at[0])
-    whole.start()
-    load = pltpu.make_async_copy(sums_ref, sums, sem.at[1])
+    chunks = [(640 * n, min(640, OWN - 640 * n)) for n in range(4)]
+    loads = [
+        pltpu.make_async_copy(
+            filtered_ref.at[pl.ds(at, rows)], held.at[pl.ds(at, rows)], sem.at[n]
+        )
+        for n, (at, rows) in enumerate(chunks)
+    ]
+    load = pltpu.make_async_copy(sums_ref, sums, sem.at[4])
     load.start()
+    for one in loads:
+        one.start()
     load.wait()
     stores = [
-        pltpu.make_async_copy(sums.at[:, pl.ds(WAVE * n, WAVE)], target, sem.at[2 + n])
+        pltpu.make_async_copy(sums.at[:, pl.ds(WAVE * n, WAVE)], target, sem.at[5 + n])
         for n, target in enumerate((corr_ref, proj_ref))
     ]
     for store in stores:
         store.start()
-    whole.wait()
-    back = pltpu.make_async_copy(held, out_ref, sem.at[4])
-    back.start()
+    for n, (at, rows) in enumerate(chunks):
+        loads[n].wait()
+        store = pltpu.make_async_copy(
+            held.at[pl.ds(at, rows)], out_ref.at[pl.ds(at, rows)], sem.at[7 + n]
+        )
+        store.start()
+        stores.append(store)
     for store in stores:
         store.wait()
-    back.wait()
 
 
 def shards(wavefunctions, cell_hamiltonian, cell_nodes, face_nodes):
@@ -720,7 +828,7 @@
             pltpu.VMEM((PAIR, 256), bf16),
             pltpu.VMEM((256, 256), bf16),
             pltpu.VMEM((OWN, WAVE), f32),
-            pltpu.VMEM((125 * CX * PAIRS, WAVE), f32),
+            pltpu.VMEM((125 * PITCH + 3, WAVE), f32),
             pltpu.VMEM((SORTED, WAVE), jnp.int32),
             pltpu.VMEM((8, SORTED), jnp.int32),
             pltpu.VMEM((GRID, WAVE), f32),
@@ -734,8 +842,8 @@
             pltpu.VMEM((CY, RUN_PAD, 256), bf16),
             pltpu.VMEM((NX, FACE_PAD, WAVE), bf16),
             pltpu.VMEM((NX, FACE_PAD, WAVE), bf16),
-            pltpu.VMEM((NX, SLAB, WAVE), bf16),
-            pltpu.VMEM((2 * NX, SLAB, WAVE), bf16),
+            pltpu.VMEM((NX, HELD, WAVE), bf16),
+            pltpu.VMEM((2 * NX, HELD, WAVE), bf16),
             pltpu.VMEM((SORTED, WAVE), bf16),
             pltpu.VMEM((OWN, WAVE), bf16),
             pltpu.VMEM((SLAB, WAVE), f32),
@@ -745,6 +853,7 @@
             pltpu.VMEM((2 * NX, 64, 2 * NX * WAVE), bf16),
             pltpu.VMEM((2 * NX, 64, 2 * NX * WAVE), bf16),
             pltpu.VMEM((2 * NX, NX, 64, 2 * WAVE), bf16),
+            pltpu.VMEM((CZ, 64, 2 * NX * WAVE), bf16),
             pltpu.VMEM((2 * NX, 64, 2 * WAVE), bf16),
             pltpu.VMEM((8, 64, 2 * WAVE), bf16),
             dma((3,)),
@@ -757,12 +866,14 @@
             dma((NX,)),
             dma((2, NX)),
             dma((2, NX)),
-            dma((2, NX)),
-            dma((2, NX)),
+            dma((NX,)),
+            dma((NX,)),
             dma((2 * NX,)),
             dma((2 * NX,)),
             dma((2 * NX, NX)),
             dma((2 * NX, NX)),
+            dma((CZ,)),
+            dma((CZ,)),
             dma((2 * NX,)),
             dma((8,)),
             dma,
@@ -786,7 +897,7 @@
         scratch_shapes=[
             pltpu.VMEM((64, 2 * WAVE), f32),
             pltpu.VMEM((OWN, WAVE), bf16),
-            dma((5,)),
+            dma((11,)),
         ],
         compiler_params=pltpu.CompilerParams(vmem_limit_bytes=63 << 20),
         name="finish",

time: 53.8 us -> 52.7 us (0.980)
  Pallas kernels: 53 us -> 51.4 us
    pallas_call x1, Pallas kernels: 51 us -> 49.5 us  [shards(): pl.pallas_call(kernel, out_shape=(jax.ShapeDtypeStruct((OWN, WAVE), bf16)...]
where the time goes in v3:
time: 52.7 us; the launch traced here: 52.1 us
  Pallas kernels  51.4 us (98%)
  between operations  0.64 us (1%)
    pallas_call x1, Pallas kernels, shards(): pl.pallas_call(kernel, out_shape=(jax.ShapeDtypeStruct((OWN, WAVE), bf16)...  49.5 us
    pallas_call x1, Pallas kernels, shards(): pl.pallas_call(finish, out_shape=(jax.ShapeDtypeStruct((OWN, WAVE), bf16)...  1.93 us

profile of v3, /device:TPU:12, one launch (start us, length us, event | category | flops | bytes accessed | tf_op | source)
XLA Modules:
  0.0 52.1 jit_solution(3809251947229222153)
XLA Ops:
  0.6 49.5 %chebyshev_filter.1 = (bf16[2448,128]{1,0:T(8,128)(2,1)}, f32[64,256]{1,0:T(8,128)}) custom-call(bf16[2448,128]{1,0:T(8,128)(2,1)} %w_hbm.1, bf16[4000,125]{1,0:T(8,128)(2,1)} %bitcast.4, s32[4,8,125]{2,1,0:T(8,128)} %bitcast.5, bf16[240,256]{1,0:T(8,128)(2,1)} %constant.4.clone.e_hbm, bf16[256,256]{1,0:T(8,128)(2,1)} %constant.5.clone.et_hbm), custom_call_target="tpu_custom_call" | custom-call | tf_op jit(solution)/shard_map/chebyshev_filter/pallas_call | solution.py:816
  50.1 1.9 %finish.1 = (bf16[2448,128]{1,0:T(8,128)(2,1)}, f32[64,128]{1,0:T(8,128)}, f32[64,128]{1,0:T(8,128)}) custom-call(bf16[2448,128]{1,0:T(8,128)(2,1)} %get-tuple-element.5.filtered_ref, f32[64,256]{1,0:T(8,128)} %get-tuple-element.6.sums_ref), custom_call_target="tpu_custom_call" | custom-call | tf_op jit(solution)/shard_map/finish/pallas_call | solution.py:888
